TPU v7x, 128 devices: a whole 4x4x4 slice. The times are simulated.
128 devices in a mesh: row: 8 (over x, y_hi), col: 16 (over y_lo, z, core).
Axes of the slice: x: 4, y: 4 (y_hi: 2, y_lo: 2; y = y_hi * 2 + y_lo), z: 4, core: 2. Of those that a mesh axis runs over, the one named last changes fastest.
Arguments:
- coupling: bfloat16 [32768, 32768], P('row', 'col'), may hold values from -0.03125 to 0.03125
- amplitude: float32 [64, 32768], P(None, 'col'), may hold values from -0.95 to 0.95
- target: float32 [64, 32768], P(None, 'col'), may hold values from -6 to 6
- shadow_target: float32 [64, 32768], P(None, 'col'), may hold values from -10.2 to 10.2
Outputs:
- solution: float32 [64, 32768], P(None, 'col')
- shadow_solution: float32 [64, 32768], P(None, 'col')
- residual: float32 [64, 32768], P(None, 'col')
- shadow_residual: float32 [64, 32768], P(None, 'col')
All inputs are finite; a program needn't handle non-finite values.
Results may differ from a plain program's by a relative error of at most 0.0036.
Values may be sent and summed in bfloat16 or wider, within the bound.
No kernel may reach another device: no remote copies, remote signals or barrier semaphores. Data moves between devices by JAX's collectives and lax.ppermute only.
A program may use at most 128 MiB of HBM per device.

v0:
```python
import jax
import jax.numpy as jnp
from jax import lax
from jax.sharding import PartitionSpec as P

ITERS = 2
SELF_GAIN = 0.5
COUPLE_GAIN = 0.3


def on_device(coupling, amplitude, target, shadow_target):
    row_rows = coupling.shape[0]
    col_rows = coupling.shape[1]
    row_index = lax.axis_index("row")
    col_index = lax.axis_index("col")
    slope = 1.0 - amplitude * amplitude
    solution = jnp.zeros_like(target)
    shadow_solution = jnp.zeros_like(target)
    residual = target
    shadow_residual = shadow_target
    direction = target
    shadow_direction = shadow_target
    align = lax.psum(jnp.sum(shadow_residual * residual, axis=1), "col")
    for iteration in range(ITERS):
        scaled = (slope * direction).astype(jnp.bfloat16)
        primary_gathered = lax.all_gather(scaled, "col", axis=1, tiled=True)
        row_block = lax.dynamic_slice_in_dim(primary_gathered, row_index * row_rows, row_rows, 1)
        primary_partial_value = jnp.dot(row_block, coupling, preferred_element_type=jnp.float32)
        product = lax.psum(primary_partial_value, "row")
        image = direction - SELF_GAIN * slope * direction - COUPLE_GAIN * product
        shadow_scaled = shadow_direction.astype(jnp.bfloat16)
        partial_value = lax.dot_general(
            shadow_scaled, coupling, (((1,), (1,)), ((), ())), preferred_element_type=jnp.float32
        )
        summed = lax.psum(partial_value, "col")
        gathered = lax.all_gather(summed, "row", axis=1, tiled=True)
        own_block = lax.dynamic_slice_in_dim(gathered, col_index * col_rows, col_rows, 1)
        shadow_image = (
            shadow_direction
            - SELF_GAIN * slope * shadow_direction
            - COUPLE_GAIN * slope * own_block
        )
        curve = lax.psum(jnp.sum(shadow_direction * image, axis=1), "col")
        step_size = align / curve
        column_step = step_size[:, None]
        solution = solution + column_step * direction
        shadow_solution = shadow_solution + column_step * shadow_direction
        residual = residual - column_step * image
        shadow_residual = shadow_residual - column_step * shadow_image
        if iteration + 1 < ITERS:
            align_next = lax.psum(jnp.sum(shadow_residual * residual, axis=1), "col")
        if iteration + 1 < ITERS:
            blend = (align_next / align)[:, None]
            direction = residual + blend * direction
            shadow_direction = shadow_residual + blend * shadow_direction
            align = align_next
    return (solution, shadow_solution, residual, shadow_residual)


def solution(mesh):
    return jax.shard_map(
        on_device,
        mesh=mesh,
        in_specs=(P("row", "col"), P(None, "col"), P(None, "col"), P(None, "col")),
        out_specs=(P(None, "col"), P(None, "col"), P(None, "col"), P(None, "col")),
        check_vma=False,
    )
```

profile of v0, /device:TPU:1, one launch (start us, length us, event | category | flops | bytes accessed | tf_op | source)
XLA Modules:
  0.0 766.5 jit_solution(14258358741011477803)
XLA Ops:
  7.2 0.0 all-gather.5.cloned.1.call-start
  7.2 2.1 multiply_convert_fusion.1
  9.3 0.0 all-gather.5.cloned.1.call-update
  9.3 0.0 all-reduce.8.cloned.1.call-start
  9.4 12.1 %fusion.14 = f32[64,4096]{1,0:T(8,128)} fusion(bf16[4096,2048]{1,0:T(8,128)(2,1)} %param.4, f32[64,2048]{1,0:T(8,128)} %param.7), kind=kOutput, calls=%fused_computation.31 | convolution fusion | flops 1073872896 | bytes 18350080 | tf_op jit(solution)/shard_map/dot_general | solution.py:32
  21.5 0.0 copy-start
  21.5 0.0 copy-start.1
  21.5 0.0 copy-start.2
  21.5 0.0 all-reduce.8.cloned.1.call-update
  21.5 0.0 all-reduce.6.cloned.1.call-start
  21.6 29.8 %all-gather.5.cloned.1.call-done = bf16[64,32768]{1,0:T(8,128)(2,1)} async-done(((bf16[64,2048]{1,0:T(8,128)(2,1)}), bf16[64,32768]{1,0:T(8,128)(2,1)}) %all-gather.5.cloned.1.call-update) | async-done | bytes 4194320 | tf_op jit(solution)/shard_map/all_gather | solution.py:26
  51.3 9.8 %fusion.10 = f32[64,2048]{1,0:T(8,128)} fusion(bf16[4096,2048]{1,0:T(8,128)(2,1)} %param.4, bf16[64,32768]{1,0:T(8,128)(2,1)} %all-gather.5.cloned.1.call-done, s32[]{:T(128)S(6)} %select_n.8), kind=kOutput, calls=%fused_computation.24 | convolution fusion | flops 1073741824 | bytes 17825796 | tf_op jit(solution)/shard_map/dot_general | solution.py:28
  61.1 0.0 all-reduce.6.cloned.1.call-update
  61.1 0.0 all-gather.7.cloned.1.call-start
  61.2 111.6 %all-reduce.8.cloned.1.call-done = f32[64,4096]{1,0:T(8,128)} async-done(((f32[64,4096]{1,0:T(8,128)}), f32[64,4096]{1,0:T(8,128)}) %all-reduce.8.cloned.1.call-update) | async-done | bytes 1048592 | tf_op jit(solution)/shard_map/psum | solution.py:35
  172.8 0.0 all-gather.7.cloned.1.call-update
  172.8 0.0 all-gather.9.cloned.1.call-start
  172.9 84.5 %all-reduce.6.cloned.1.call-done = f32[64,2048]{1,0:T(8,128)} async-done(((f32[64,2048]{1,0:T(8,128)}), f32[64,2048]{1,0:T(8,128)}) %all-reduce.6.cloned.1.call-update) | async-done | bytes 524304 | tf_op jit(solution)/shard_map/psum | solution.py:29
  257.3 0.0 copy-done
  257.3 0.0 copy-done.1
  257.3 0.0 copy-done.2
  257.3 1.3 multiply_reduce_fusion.2
  258.7 32.6 %all-reduce = (f32[64]{0:T(128)S(1)}, f32[64]{0:T(128)S(1)}) all-reduce(f32[64]{0:T(128)S(1)} %get-tuple-element.5, f32[64]{0:T(128)S(1)} %get-tuple-element.4), channel_id=1, replica_groups=mesh['row'=8,'col'=16] {'col'}, use_global_device_ids=true, to_apply=%region_1.0 | all-reduce | flops 128 | bytes 1024 | tf_op jit(solution)/shard_map/psum | solution.py:23
  291.3 79.8 %all-gather.7.cloned.1.call-done = f32[64,32768]{1,0:T(8,128)} async-done(((f32[64,4096]{1,0:T(8,128)}), f32[64,32768]{1,0:T(8,128)}) %all-gather.7.cloned.1.call-update) | async-done | bytes 8388624 | tf_op jit(solution)/shard_map/all_gather | solution.py:36
  371.0 1.6 multiply_reduce_fusion.1
  372.7 27.6 %psum.60 = f32[64]{0:T(128)S(1)} all-reduce(f32[64]{0:T(128)S(1)} %get-tuple-element.10), channel_id=1, replica_groups=mesh['row'=8,'col'=16] {'col'}, use_global_device_ids=true, to_apply=%region_7.0 | all-reduce | flops 64 | bytes 512 | tf_op jit(solution)/shard_map/psum | solution.py:51
  400.3 0.9 multiply_convert_fusion
  401.1 0.0 all-gather.9.cloned.1.call-update
  401.1 0.0 all-reduce.12.cloned.1.call-start
  401.2 12.0 %fusion.12 = f32[64,4096]{1,0:T(8,128)} fusion(bf16[4096,2048]{1,0:T(8,128)(2,1)} %param.4, f32[64,2048]{1,0:T(8,128)S(1)} %get-tuple-element.12, f32[64,2048]{1,0:T(8,128)S(1)} %copy-done, f32[64]{0:T(128)S(1)} %div.10), kind=kOutput, calls=%fused_computation.29 | convolution fusion | flops 1074135040 | bytes 18874624 | tf_op jit(solution)/shard_map/dot_general | solution.py:32
  413.2 0.0 all-reduce.12.cloned.1.call-update
  413.2 0.2 all-reduce.10.cloned.1.call-start
  413.4 23.9 %all-gather.9.cloned.1.call-done = bf16[64,32768]{1,0:T(8,128)(2,1)} async-done(((bf16[64,2048]{1,0:T(8,128)(2,1)}), bf16[64,32768]{1,0:T(8,128)(2,1)}) %all-gather.9.cloned.1.call-update) | async-done | bytes 4194320 | tf_op jit(solution)/shard_map/all_gather | solution.py:26
  437.4 9.8 %fusion.8 = f32[64,2048]{1,0:T(8,128)} fusion(bf16[4096,2048]{1,0:T(8,128)(2,1)} %param.4, bf16[64,32768]{1,0:T(8,128)(2,1)} %all-gather.9.cloned.1.call-done, s32[]{:T(128)S(6)} %select_n.8), kind=kOutput, calls=%fused_computation.16 | convolution fusion | flops 1073741824 | bytes 17825796 | tf_op jit(solution)/shard_map/dot_general | solution.py:28
  447.1 0.0 all-reduce.10.cloned.1.call-update
  447.1 0.0 all-gather.11.cloned.1.call-start
  447.2 111.4 %all-reduce.12.cloned.1.call-done = f32[64,4096]{1,0:T(8,128)} async-done(((f32[64,4096]{1,0:T(8,128)}), f32[64,4096]{1,0:T(8,128)}) %all-reduce.12.cloned.1.call-update) | async-done | bytes 1048592 | tf_op jit(solution)/shard_map/psum | solution.py:35
  558.6 0.0 all-gather.11.cloned.1.call-update
  558.7 84.5 %all-reduce.10.cloned.1.call-done = f32[64,2048]{1,0:T(8,128)} async-done(((f32[64,2048]{1,0:T(8,128)}), f32[64,2048]{1,0:T(8,128)}) %all-reduce.10.cloned.1.call-update) | async-done | bytes 524304 | tf_op jit(solution)/shard_map/psum | solution.py:29
  643.2 1.4 multiply_reduce_fusion
  644.6 32.6 %psum.62 = f32[64]{0:T(128)S(1)} all-reduce(f32[64]{0:T(128)S(1)} %get-tuple-element.8), channel_id=1, replica_groups=mesh['row'=8,'col'=16] {'col'}, use_global_device_ids=true, to_apply=%region_10.0 | all-reduce | flops 64 | bytes 512 | tf_op jit(solution)/shard_map/psum | solution.py:43
  677.2 79.8 %all-gather.11.cloned.1.call-done = f32[64,32768]{1,0:T(8,128)} async-done(((f32[64,4096]{1,0:T(8,128)}), f32[64,32768]{1,0:T(8,128)}) %all-gather.11.cloned.1.call-update) | async-done | bytes 8388624 | tf_op jit(solution)/shard_map/all_gather | solution.py:36
  757.0 2.7 multiply_subtract_fusion.4
  (3 shorter events, 0.0 us)
Async XLA Ops:
  7.2 44.2 %all-gather.5.cloned.1.call-start = ((), (), s32[]{:S(2)}) async-start(), calls=%async_computation | async-start | bytes 4456448 | tf_op jit(solution)/shard_map/all_gather | solution.py:26
  9.3 163.5 %all-reduce.8.cloned.1.call-start = ((), (), s32[]{:S(2)}) async-start(), calls=%async_computation.2 | async-start | bytes 2097152 | tf_op jit(solution)/shard_map/psum | solution.py:35
  21.5 235.8 %copy-start = (f32[64,2048]{1,0:T(8,128)S(1)}, f32[64,2048]{1,0:T(8,128)}, u32[]{:S(2)}) copy-start(f32[64,2048]{1,0:T(8,128)} %param.7) | copy-start | bytes 1572868
  21.5 235.8 %copy-start.1 = (f32[64,2048]{1,0:T(8,128)S(1)}, f32[64,2048]{1,0:T(8,128)}, u32[]{:S(2)}) copy-start(f32[64,2048]{1,0:T(8,128)} %param.6) | copy-start | bytes 1572868
  21.5 235.8 %copy-start.2 = (f32[64,2048]{1,0:T(8,128)S(1)}, f32[64,2048]{1,0:T(8,128)}, u32[]{:S(2)}) copy-start(f32[64,2048]{1,0:T(8,128)} %param.5) | copy-start | bytes 1572868
  21.5 235.8 %all-reduce.6.cloned.1.call-start = ((), (), s32[]{:S(2)}) async-start(), calls=%async_computation.1 | async-start | bytes 1048576 | tf_op jit(solution)/shard_map/psum | solution.py:29
  61.1 309.9 %all-gather.7.cloned.1.call-start = ((), (), s32[]{:S(2)}) async-start(), calls=%async_computation.3 | async-start | bytes 9437184 | tf_op jit(solution)/shard_map/all_gather | solution.py:36
  172.8 264.5 %all-gather.9.cloned.1.call-start = ((), (), s32[]{:S(2)}) async-start(), calls=%async_computation.4 | async-start | bytes 4456448 | tf_op jit(solution)/shard_map/all_gather | solution.py:26
  401.1 157.5 %all-reduce.12.cloned.1.call-start = ((), (), s32[]{:S(2)}) async-start(), calls=%async_computation.6 | async-start | bytes 2097152 | tf_op jit(solution)/shard_map/psum | solution.py:35
  413.2 230.0 %all-reduce.10.cloned.1.call-start = ((), (), s32[]{:S(2)}) async-start(), calls=%async_computation.5 | async-start | bytes 1048576 | tf_op jit(solution)/shard_map/psum | solution.py:29
  447.1 309.9 %all-gather.11.cloned.1.call-start = ((), (), s32[]{:S(2)}) async-start(), calls=%async_computation.7 | async-start | bytes 9437184 | tf_op jit(solution)/shard_map/all_gather | solution.py:36
Sparse Core Ops, SparseCore 0:
  10.2 41.0 all-gather.4
  53.8 118.9 all-reduce.7
  176.0 81.2 all-reduce.5
  259.5 111.4 all-gather.6
  401.2 36.0 all-gather.8
  439.7 118.9 all-reduce.11
  561.9 81.2 all-reduce.9
  645.5 111.4 all-gather.10
where the time goes:
time: 767 us
  waiting for transfers between devices  605 us (79%)
  blocking collectives  92.8 us (12%)
  matrix products  43.6 us (6%)
  between operations  14.2 us (2%)
  other arithmetic  10 us (1%)
    psum x2, waiting for transfers between devices, on_device(): summed = lax.psum(partial_value, 'col')  223 us
    psum x2, waiting for transfers between devices, on_device(): product = lax.psum(primary_partial_value, 'row')  169 us
    all_gather x2, waiting for transfers between devices, on_device(): gathered = lax.all_gather(summed, 'row', axis=1, tiled=True)  160 us
    all_gather x2, waiting for transfers between devices, on_device(): primary_gathered = lax.all_gather(scaled, 'col', axis=1, tiled=True)  53.7 us
    psum x1, blocking collectives, on_device(): curve = lax.psum(jnp.sum(shadow_direction * image, axis=1), 'col')  32.6 us
    psum x1, blocking collectives, on_device(): align = lax.psum(jnp.sum(shadow_residual * residual, axis=1), 'col')  32.6 us
    psum x1, blocking collectives, on_device(): align_next = lax.psum(jnp.sum(shadow_residual * residual, axis=1), 'col')  27.6 us
    dot_general x2, matrix products, on_device(): lax.dot_general(shadow_scaled, coupling, (((1,), (1,)), ((), ())), prefer...  24.1 us
  transfers between devices with their start and end apart: 8, of which 8 were waited for; matrix products, arithmetic and copies ran while one was open for 6% of the time, Pallas kernels for 0%

commit v1 on v0

--- a/solution.py
+++ b/solution.py
@@ -33,7 +33,9 @@
             shadow_scaled, coupling, (((1,), (1,)), ((), ())), preferred_element_type=jnp.float32
         )
         summed = lax.psum(partial_value, "col")
-        gathered = lax.all_gather(summed, "row", axis=1, tiled=True)
+        gathered = jnp.concatenate(
+            lax.all_to_all(jnp.stack([summed] * lax.axis_size("row")), "row", 0, 0), axis=1
+        )
         own_block = lax.dynamic_slice_in_dim(gathered, col_index * col_rows, col_rows, 1)
         shadow_image = (
             shadow_direction

time: 767 us -> 801 us (1.044)
  local copies, waits for them, and re-layouts: 0.01 us -> 26.3 us
  starting transfers between devices: 0.51 us -> 12.7 us
    all_gather x2, waiting for transfers between devices: 53.7 us -> 222 us  [on_device(): primary_gathered = lax.all_gather(scaled, 'col', axis=1, tiled=True)]
    all_gather x2 -> x0, waiting for transfers between devices: 160 us -> none  [on_device(): gathered = lax.all_gather(summed, 'row', axis=1, tiled=True)]
    psum x2, waiting for transfers between devices: 169 us -> 144 us  [on_device(): product = lax.psum(primary_partial_value, 'row')]
    reshape x0 -> x2, local copies, waits for them, and re-layouts: none -> 15.2 us  [on_device(): jnp.concatenate(lax.all_to_all(jnp.stack([summed] * lax.axis_size('row'))...]
    psum x2, waiting for transfers between devices: 223 us -> 236 us  [on_device(): summed = lax.psum(partial_value, 'col')]
    all_to_all x0 -> x2, starting transfers between devices: none -> 12.3 us  [on_device(): lax.all_to_all(jnp.stack([summed] * lax.axis_size('row')), 'row', 0, 0)]
    another operation x0 -> x2, local copies, waits for them, and re-layouts: none -> 11 us  [on_device(): jnp.stack([summed] * lax.axis_size('row'))]
  transfers between devices with their start and end apart: 8 -> 8, of which waited for: 8 -> 6; matrix products, arithmetic and copies ran while one was open for 6% -> 6% of each run, Pallas kernels for 0% -> 0%
where the time goes in v1:
time: 801 us; the launch traced here: 800 us
  waiting for transfers between devices  603 us (75%)
  blocking collectives  91.9 us (11%)
  matrix products  43.8 us (5%)
  local copies, waits for them, and re-layouts  26.3 us (3%)
  between operations  14.2 us (2%)
  starting transfers between devices  12.7 us (2%)
  other arithmetic  8.68 us (1%)
    psum x2, waiting for transfers between devices, on_device(): summed = lax.psum(partial_value, 'col')  236 us
    all_gather x2, waiting for transfers between devices, on_device(): primary_gathered = lax.all_gather(scaled, 'col', axis=1, tiled=True)  222 us
    psum x2, waiting for transfers between devices, on_device(): product = lax.psum(primary_partial_value, 'row')  144 us
    psum x1, blocking collectives, on_device(): align = lax.psum(jnp.sum(shadow_residual * residual, axis=1), 'col')  32.4 us
    psum x1, blocking collectives, on_device(): curve = lax.psum(jnp.sum(shadow_direction * image, axis=1), 'col')  32.4 us
    psum x1, blocking collectives, on_device(): align_next = lax.psum(jnp.sum(shadow_residual * residual, axis=1), 'col')  27.1 us
    dot_general x2, matrix products, on_device(): lax.dot_general(shadow_scaled, coupling, (((1,), (1,)), ((), ())), prefer...  24.3 us
    dot_general x2, matrix products, on_device(): jnp.dot(row_block, coupling, preferred_element_type=jnp.float32)  19.5 us
  transfers between devices with their start and end apart: 8, of which 6 were waited for; matrix products, arithmetic and copies ran while one was open for 6% of the time, Pallas kernels for 0%

profile of v1, /device:TPU:1, one launch (start us, length us, event | category | flops | bytes accessed | tf_op | source)
XLA Modules:
  0.0 800.1 jit_solution(9298472651001695556)
XLA Ops:
  7.2 0.0 copy-start.2
  7.2 0.0 copy-start.1
  7.2 0.0 all-reduce.8.cloned.1.call-start
  7.2 12.2 %fusion.14 = f32[64,4096]{1,0:T(8,128)} fusion(bf16[4096,2048]{1,0:T(8,128)(2,1)} %param.4, f32[64,2048]{1,0:T(8,128)} %param.7), kind=kOutput, calls=%fused_computation.31 | convolution fusion | flops 1073872896 | bytes 18350080 | tf_op jit(solution)/shard_map/dot_general | solution.py:32
  19.5 0.0 all-reduce.8.cloned.1.call-update
  19.5 0.0 all-gather.3.cloned.1.call-start
  19.5 0.0 copy-done.2
  19.5 0.0 copy-done.1
  19.6 0.8 multiply_convert_fusion.1
  20.3 0.0 all-gather.3.cloned.1.call-update
  20.3 122.1 %all-reduce.8.cloned.1.call-done = f32[64,4096]{1,0:T(8,128)} async-done(((f32[64,4096]{1,0:T(8,128)}), f32[64,4096]{1,0:T(8,128)}) %all-reduce.8.cloned.1.call-update) | async-done | bytes 1048592 | tf_op jit(solution)/shard_map/psum | solution.py:35
  142.4 5.5 stack.4
  148.0 6.1 all-to-all-start
  154.1 0.0 all-reduce.6.cloned.1.call-start
  154.1 111.1 %all-gather.3.cloned.1.call-done = bf16[64,32768]{1,0:T(8,128)(2,1)} async-done(((bf16[64,2048]{1,0:T(8,128)(2,1)}), bf16[64,32768]{1,0:T(8,128)(2,1)}) %all-gather.3.cloned.1.call-update) | async-done | bytes 4194320 | tf_op jit(solution)/shard_map/all_gather | solution.py:26
  265.2 9.8 %fusion.10 = f32[64,2048]{1,0:T(8,128)} fusion(bf16[4096,2048]{1,0:T(8,128)(2,1)} %param.4, bf16[64,32768]{1,0:T(8,128)(2,1)} %all-gather.3.cloned.1.call-done, s32[]{:T(128)S(6)} %select_n.8), kind=kOutput, calls=%fused_computation.24 | convolution fusion | flops 1073741824 | bytes 17825796 | tf_op jit(solution)/shard_map/dot_general | solution.py:28
  275.0 0.0 all-reduce.6.cloned.1.call-update
  275.0 0.0 all-reduce.12.cloned.1.call-start
  275.1 0.0 all-to-all-done
  275.1 0.0 copy-start
  275.1 7.6 copy.10
  282.8 72.1 %all-reduce.6.cloned.1.call-done = f32[64,2048]{1,0:T(8,128)} async-done(((f32[64,2048]{1,0:T(8,128)}), f32[64,2048]{1,0:T(8,128)}) %all-reduce.6.cloned.1.call-update) | async-done | bytes 524304 | tf_op jit(solution)/shard_map/psum | solution.py:29
  354.8 0.0 copy-done
  354.8 1.3 multiply_reduce_fusion.2
  356.2 32.4 %all-reduce = (f32[64]{0:T(128)S(1)}, f32[64]{0:T(128)S(1)}) all-reduce(f32[64]{0:T(128)S(1)} %get-tuple-element.5, f32[64]{0:T(128)S(1)} %get-tuple-element.4), channel_id=1, replica_groups=mesh['row'=8,'col'=16] {'col'}, use_global_device_ids=true, to_apply=%region_1.0 | all-reduce | flops 128 | bytes 1024 | tf_op jit(solution)/shard_map/psum | solution.py:23
  388.6 1.6 multiply_reduce_fusion.1
  390.2 27.1 %psum.60 = f32[64]{0:T(128)S(1)} all-reduce(f32[64]{0:T(128)S(1)} %get-tuple-element.10), channel_id=1, replica_groups=mesh['row'=8,'col'=16] {'col'}, use_global_device_ids=true, to_apply=%region_7.0 | all-reduce | flops 64 | bytes 512 | tf_op jit(solution)/shard_map/psum | solution.py:53
  417.3 12.0 %fusion.12 = f32[64,4096]{1,0:T(8,128)} fusion(bf16[4096,2048]{1,0:T(8,128)(2,1)} %param.4, f32[64,2048]{1,0:T(8,128)S(1)} %get-tuple-element.12, f32[64,2048]{1,0:T(8,128)S(1)} %copy-done, f32[64]{0:T(128)S(1)} %div.10), kind=kOutput, calls=%fused_computation.29 | convolution fusion | flops 1074135040 | bytes 18874624 | tf_op jit(solution)/shard_map/dot_general | solution.py:32
  429.4 0.0 all-reduce.12.cloned.1.call-update
  429.4 0.2 all-gather.5.cloned.1.call-start
  429.6 0.8 multiply_convert_fusion
  430.5 0.0 all-gather.5.cloned.1.call-update
  430.5 113.9 %all-reduce.12.cloned.1.call-done = f32[64,4096]{1,0:T(8,128)} async-done(((f32[64,4096]{1,0:T(8,128)}), f32[64,4096]{1,0:T(8,128)}) %all-reduce.12.cloned.1.call-update) | async-done | bytes 1048592 | tf_op jit(solution)/shard_map/psum | solution.py:35
  544.4 5.5 stack.5
  549.9 6.1 all-to-all-start.1
  556.0 0.0 all-reduce.10.cloned.1.call-start
  556.1 111.1 %all-gather.5.cloned.1.call-done = bf16[64,32768]{1,0:T(8,128)(2,1)} async-done(((bf16[64,2048]{1,0:T(8,128)(2,1)}), bf16[64,32768]{1,0:T(8,128)(2,1)}) %all-gather.5.cloned.1.call-update) | async-done | bytes 4194320 | tf_op jit(solution)/shard_map/all_gather | solution.py:26
  667.2 9.8 %fusion.8 = f32[64,2048]{1,0:T(8,128)} fusion(bf16[4096,2048]{1,0:T(8,128)(2,1)} %param.4, bf16[64,32768]{1,0:T(8,128)(2,1)} %all-gather.5.cloned.1.call-done, s32[]{:T(128)S(6)} %select_n.8), kind=kOutput, calls=%fused_computation.16 | convolution fusion | flops 1073741824 | bytes 17825796 | tf_op jit(solution)/shard_map/dot_general | solution.py:28
  677.0 0.0 all-reduce.10.cloned.1.call-update
  677.0 0.0 all-to-all-done.1
  677.0 7.6 copy.11
  684.6 72.2 %all-reduce.10.cloned.1.call-done = f32[64,2048]{1,0:T(8,128)} async-done(((f32[64,2048]{1,0:T(8,128)}), f32[64,2048]{1,0:T(8,128)}) %all-reduce.10.cloned.1.call-update) | async-done | bytes 524304 | tf_op jit(solution)/shard_map/psum | solution.py:29
  756.8 1.4 multiply_reduce_fusion
  758.2 32.4 %psum.62 = f32[64]{0:T(128)S(1)} all-reduce(f32[64]{0:T(128)S(1)} %get-tuple-element.8), channel_id=1, replica_groups=mesh['row'=8,'col'=16] {'col'}, use_global_device_ids=true, to_apply=%region_10.0 | all-reduce | flops 64 | bytes 512 | tf_op jit(solution)/shard_map/psum | solution.py:45
  790.6 2.7 multiply_subtract_fusion.4
  (3 shorter events, 0.0 us)
Async XLA Ops:
  7.2 12.4 %copy-start.2 = (f32[64,2048]{1,0:T(8,128)S(1)}, f32[64,2048]{1,0:T(8,128)}, u32[]{:S(2)}) copy-start(f32[64,2048]{1,0:T(8,128)} %param.5) | copy-start | bytes 1572868
  7.2 12.4 %copy-start.1 = (f32[64,2048]{1,0:T(8,128)S(1)}, f32[64,2048]{1,0:T(8,128)}, u32[]{:S(2)}) copy-start(f32[64,2048]{1,0:T(8,128)} %param.6) | copy-start | bytes 1572868
  7.2 135.3 %all-reduce.8.cloned.1.call-start = ((), (), s32[]{:S(2)}) async-start(), calls=%async_computation.4 | async-start | bytes 2097152 | tf_op jit(solution)/shard_map/psum | solution.py:35
  19.5 245.8 %all-gather.3.cloned.1.call-start = ((), (), s32[]{:S(2)}) async-start(), calls=%async_computation.2 | async-start | bytes 4456448 | tf_op jit(solution)/shard_map/all_gather | solution.py:26
  148.0 127.1 %all-to-all-start = ((f32[8,64,4096]{2,1,0:T(8,128)}), f32[8,64,4096]{2,1,0:T(8,128)}, u32[]{:S(2)}, u32[]{:S(2)}) async-start(f32[8,64,4096]{2,1,0:T(8,128)} %stack.4), calls=%async_computation | async-start | bytes 16777216 | tf_op jit(solution)/shard_map/all_to_all | solution.py:37
  154.1 200.7 %all-reduce.6.cloned.1.call-start = ((), (), s32[]{:S(2)}) async-start(), calls=%async_computation.3 | async-start | bytes 1048576 | tf_op jit(solution)/shard_map/psum | solution.py:29
  275.0 269.3 %all-reduce.12.cloned.1.call-start = ((), (), s32[]{:S(2)}) async-start(), calls=%async_computation.7 | async-start | bytes 2097152 | tf_op jit(solution)/shard_map/psum | solution.py:35
  275.1 79.7 %copy-start = (f32[64,2048]{1,0:T(8,128)S(1)}, f32[64,2048]{1,0:T(8,128)}, u32[]{:S(2)}) copy-start(f32[64,2048]{1,0:T(8,128)} %param.7) | copy-start | bytes 1572868
  429.4 237.8 %all-gather.5.cloned.1.call-start = ((), (), s32[]{:S(2)}) async-start(), calls=%async_computation.5 | async-start | bytes 4456448 | tf_op jit(solution)/shard_map/all_gather | solution.py:26
  549.9 127.1 %all-to-all-start.1 = ((f32[8,64,4096]{2,1,0:T(8,128)}), f32[8,64,4096]{2,1,0:T(8,128)}, u32[]{:S(2)}, u32[]{:S(2)}) async-start(f32[8,64,4096]{2,1,0:T(8,128)} %stack.5), calls=%async_computation.1 | async-start | bytes 16777216 | tf_op jit(solution)/shard_map/all_to_all | solution.py:37
  556.0 200.7 %all-reduce.10.cloned.1.call-start = ((), (), s32[]{:S(2)}) async-start(), calls=%async_computation.6 | async-start | bytes 1048576 | tf_op jit(solution)/shard_map/psum | solution.py:29
Sparse Core Ops, SparseCore 0:
  19.6 122.7 all-reduce.7
  144.8 120.4 all-gather.2
  275.2 79.6 all-reduce.5
  429.5 114.8 all-reduce.11
  546.6 120.5 all-gather.4
  677.1 79.6 all-reduce.9
